TPU v7x, 128 devices: a whole 4x4x4 slice. The times are simulated.
128 devices in a mesh: wide: 16 (over z_hi, x, core), narrow: 8 (over z_lo, y).
Axes of the slice: x: 4, y: 4, z: 4 (z_hi: 2, z_lo: 2; z = z_hi * 2 + z_lo), core: 2. Of those that a mesh axis runs over, the one named last changes fastest.
Arguments:
- tokens: bfloat16 [1536, 8192], P('wide', 'narrow'), may hold values from -6 to 6
- gate_up: bfloat16 [2, 28672, 8192], P(None, ('narrow', 'wide')), may hold values from -0.0625 to 0.0625
- down_weight: bfloat16 [28672, 8192], P(('narrow', 'wide')), may hold values from -0.125 to 0.125
Outputs:
- ffn_out: float32 [1536, 8192], P('wide', 'narrow')
All inputs are finite; a program needn't handle non-finite values.
Results may differ from a plain program's by a relative error of at most 0.0029.
Values may be sent and summed in bfloat16 or wider, within the bound.
No kernel may reach another device: no remote copies, remote signals or barrier semaphores. Data moves between devices by JAX's collectives and lax.ppermute only.
A program may use at most 192 MiB of HBM per device.

v0:
```python
import jax
import jax.numpy as jnp
from jax import lax
from jax.sharding import PartitionSpec as P


def activate(gate_sum, up_sum):
    return (jax.nn.silu(gate_sum) * up_sum).astype(jnp.bfloat16)


def shards(tokens, gate_up, down_weight):
    tok_rows = lax.all_gather(tokens, "wide", axis=0, tiled=True)
    blocks = (
        lax.all_to_all(
            lax.all_to_all(gate_up, "wide", split_axis=1, concat_axis=1, tiled=True),
            "narrow",
            split_axis=2,
            concat_axis=1,
            tiled=True,
        ),
        lax.all_to_all(
            lax.all_to_all(down_weight[None], "wide", split_axis=1, concat_axis=1, tiled=True),
            "narrow",
            split_axis=2,
            concat_axis=1,
            tiled=True,
        ),
    )
    gate_up_block = blocks[0]
    down_block = blocks[1][0]
    hid_width = gate_up_block.shape[1]
    flat_weights = gate_up_block.reshape(2 * hid_width, gate_up_block.shape[2])
    partial_sums = lax.psum_scatter(
        lax.dot_general(
            tok_rows, flat_weights, (((1,), (1,)), ((), ())), preferred_element_type=jnp.float32
        ),
        "narrow",
        scatter_dimension=0,
        tiled=True,
    )
    hidden = activate(partial_sums[:, :hid_width], partial_sums[:, hid_width:])
    down_part = jnp.dot(
        lax.all_gather(hidden, "narrow", axis=0, tiled=True),
        down_block,
        preferred_element_type=jnp.float32,
    )
    return lax.psum_scatter(down_part, "wide", scatter_dimension=0, tiled=True)


def solution(mesh):
    return jax.shard_map(
        shards,
        mesh=mesh,
        in_specs=(
            P("wide", "narrow"),
            P(None, ("narrow", "wide"), None),
            P(("narrow", "wide"), None),
        ),
        out_specs=P("wide", "narrow"),
        check_vma=False,
    )
```

profile of v0, /device:TPU:1, one launch (start us, length us, event | category | flops | bytes accessed | tf_op | source)
XLA Modules:
  0.0 917.4 jit_solution(14386936669119227121)
XLA Ops:
  6.5 12.8 %copy.13 = bf16[2,224,8192]{2,0,1:T(2,128)(2,1)S(1)} copy(bf16[2,224,8192]{2,1,0:T(8,128)(2,1)} %param.4) | data formatting | bytes 14680064 | tf_op args[1]
  19.4 93.4 %all_to_all.40 = bf16[2,224,8192]{2,0,1:T(2,128)(2,1)} all-to-all(bf16[2,224,8192]{2,0,1:T(2,128)(2,1)S(1)} %copy.13), channel_id=1, replica_groups=mesh['wide'=16,'narrow'=8] {'wide'}, dimensions={1} | all-to-all | bytes 14680064 | tf_op jit(solution)/shard_map/all_to_all | solution.py:15
  112.8 28.4 %copy.14 = bf16[2,224,8192]{1,0,2:T(2,128)(2,1)} copy(bf16[2,224,8192]{2,0,1:T(2,128)(2,1)} %all_to_all.40) | data formatting | bytes 14680064 | tf_op jit(solution)/shard_map/all_to_all | solution.py:15
  141.2 4.9 all-to-all-start.1
  146.2 0.0 all-gather.3.cloned.1.call-start
  146.2 0.7 all-gather.3.cloned.1.call-update
  146.9 0.0 reduce-scatter.3.cloned.1.call-start
  147.0 93.7 %all-to-all-done.1 = bf16[2,224,8192]{1,0,2:T(2,128)(2,1)} async-done(((bf16[2,224,8192]{1,0,2:T(2,128)(2,1)}), bf16[2,224,8192]{1,0,2:T(2,128)(2,1)}, u32[]{:S(2)}, u32[]{:S(2)}) %all-to-all-start.1) | async-done | bytes 7340064 | tf_op jit(solution)/shard_map/all_to_all | solution.py:14
  240.6 21.0 %copy.22 = bf16[2,224,8,1024]{3,1,2,0:T(8,128)(2,1)} copy(bf16[2,224,8,1024]{1,0,3,2:T(2,128)(2,1)} %bitcast) | data formatting | bytes 14680064 | tf_op jit(solution)/shard_map/all_to_all | solution.py:14
  261.6 0.0 all-gather.3.cloned.1.call-done
  261.6 18.9 %fusion.1 = f32[1536,3584]{1,0:T(8,128)} fusion(bf16[1536,1024]{1,0:T(8,128)(2,1)} %all-gather.3.cloned.1.call-done, bf16[3584,1024]{1,0:T(8,128)(2,1)} %bitcast.25), kind=kOutput, calls=%fused_computation.3 | convolution fusion | flops 11274289152 | bytes 32505856 | tf_op jit(solution)/shard_map/dot_general | solution.py:34
  280.6 0.0 reduce-scatter.3.cloned.1.call-update
  280.6 0.0 all-gather.5.cloned.1.call-start
  280.6 250.2 %reduce-scatter.3.cloned.1.call-done = f32[192,3584]{1,0:T(8,128)} async-done(((f32[1536,3584]{1,0:T(8,128)}), f32[192,3584]{1,0:T(8,128)}) %reduce-scatter.3.cloned.1.call-update) | async-done | bytes 2752528 | tf_op jit(solution)/shard_map/reduce_scatter | solution.py:33
  530.8 3.0 fusion
  533.8 0.0 all-gather.5.cloned.1.call-update
  533.9 0.0 reduce-scatter.5.cloned.1.call-start
  533.9 9.1 copy.26
  543.0 0.5 broadcast.2
  543.5 23.9 %reduce = bf16[224,8192]{1,0:T(8,128)(2,1)} reduce(bf16[224,1,8192]{2,1,0:T(2,128)(2,1)} %bitcast.21, bf16[]{:T(256)} %broadcast.2), dimensions={1}, to_apply=%bitcast.18.reduce_sub_computation | reduce | bytes 7340034
  567.4 6.4 reshape.7
  573.8 64.5 %all_to_all.41 = bf16[16,2,57344]{2,1,0:T(2,128)(2,1)} all-to-all(bf16[16,2,57344]{2,1,0:T(2,128)(2,1)} %reshape.7), channel_id=1, replica_groups=mesh['wide'=16,'narrow'=8] {'wide'}, dimensions={0} | all-to-all | bytes 7340032 | tf_op jit(solution)/shard_map/all_to_all | solution.py:22
  638.3 12.0 %reshape.8 = bf16[224,1,8192]{2,1,0:T(2,128)(2,1)} reshape(bf16[16,2,57344]{2,1,0:T(2,128)(2,1)} %all_to_all.41) | data formatting | bytes 7340032
  650.3 28.4 %copy.18 = bf16[1,224,8192]{1,0,2:T(2,128)(2,1)} copy(bf16[1,224,8192]{2,0,1:T(2,128)(2,1)} %bitcast.22) | data formatting | bytes 7340032 | tf_op jit(solution)/shard_map/all_to_all | solution.py:22
  678.7 47.6 %reduce.1 = bf16[8192,224]{1,0:T(8,128)(2,1)} reduce(bf16[8192,1,224]{2,1,0:T(2,128)(2,1)} %bitcast.19, bf16[]{:T(256)} %broadcast.2), dimensions={1}, to_apply=%bitcast.11.reduce_sub_computation | reduce | bytes 7340034
  726.3 10.0 %reshape.9 = bf16[8,2,114688]{2,1,0:T(2,128)(2,1)} reshape(bf16[8192,224]{1,0:T(8,128)(2,1)} %reduce.1) | data formatting | bytes 7340032
  736.3 48.4 %all_to_all.42 = bf16[8,2,114688]{2,1,0:T(2,128)(2,1)} all-to-all(bf16[8,2,114688]{2,1,0:T(2,128)(2,1)} %reshape.9), channel_id=1, replica_groups=mesh['wide'=16,'narrow'=8] {'narrow'}, dimensions={0} | all-to-all | bytes 7340032 | tf_op jit(solution)/shard_map/all_to_all | solution.py:21
  784.8 11.0 %reshape.10 = bf16[8192,1,224]{2,1,0:T(2,128)(2,1)} reshape(bf16[8,2,114688]{2,1,0:T(2,128)(2,1)} %all_to_all.42) | data formatting | bytes 7340032
  795.7 6.1 copy.24
  801.8 6.7 copy.23
  808.5 5.9 copy.20
  814.4 0.0 all-gather.5.cloned.1.call-done
  814.4 10.6 %fusion.2 = f32[1536,1024]{1,0:T(8,128)} fusion(bf16[1536,1792]{1,0:T(8,128)(2,1)} %all-gather.5.cloned.1.call-done, bf16[1792,1024]{1,0:T(8,128)(2,1)} %bitcast.26), kind=kOutput, calls=%fused_computation.4 | convolution fusion | flops 5637144576 | bytes 15466496 | tf_op jit(solution)/shard_map/dot_general | solution.py:42
  825.0 0.0 reduce-scatter.5.cloned.1.call-update
  825.0 85.8 %reduce-scatter.5.cloned.1.call-done = f32[96,1024]{1,0:T(8,128)} async-done(((f32[1536,1024]{1,0:T(8,128)}), f32[96,1024]{1,0:T(8,128)}) %reduce-scatter.5.cloned.1.call-update) | async-done | bytes 393232 | tf_op jit(solution)/shard_map/reduce_scatter | solution.py:47
Async XLA Ops:
  141.2 99.4 %all-to-all-start.1 = ((bf16[2,224,8192]{1,0,2:T(2,128)(2,1)}), bf16[2,224,8192]{1,0,2:T(2,128)(2,1)}, u32[]{:S(2)}, u32[]{:S(2)}) async-start(bf16[2,224,8192]{1,0,2:T(2,128)(2,1)} %copy.14), calls=%async_computation.1 | async-start | bytes 16777216 | tf_op jit(solution)/shard_map/all_to_all | solution.py:14
  146.2 115.5 %all-gather.3.cloned.1.call-start = ((), (), s32[]{:S(2)}) async-start(), calls=%async_computation.6 | async-start | bytes 3342336 | tf_op jit(solution)/shard_map/all_gather | solution.py:12
  146.9 383.9 %reduce-scatter.3.cloned.1.call-start = ((), (), s32[]{:S(2)}) async-start(), calls=%async_computation.7 | async-start | bytes 24772608 | tf_op jit(solution)/shard_map/reduce_scatter | solution.py:33
  280.6 533.9 %all-gather.5.cloned.1.call-start = ((), (), s32[]{:S(2)}) async-start(), calls=%async_computation.8 | async-start | bytes 6193152 | tf_op jit(solution)/shard_map/all_gather | solution.py:43
  533.9 377.0 %reduce-scatter.5.cloned.1.call-start = ((), (), s32[]{:S(2)}) async-start(), calls=%async_computation.9 | async-start | bytes 6684672 | tf_op jit(solution)/shard_map/reduce_scatter | solution.py:47
Sparse Core Ops, SparseCore 0:
  149.5 108.1 all-gather.2
  280.7 250.0 reduce-scatter.2
  534.0 81.0 all-gather.4
  825.2 85.6 reduce-scatter.4
where the time goes:
time: 921 us; the launch traced here: 917 us
  waiting for transfers between devices  430 us (47%)
  blocking collectives  206 us (22%)
  local copies, waits for them, and re-layouts  158 us (17%)
  other arithmetic  74.5 us (8%)
  matrix products  29.5 us (3%)
  between operations  13.2 us (1%)
    reduce_scatter x1, waiting for transfers between devices, shards(): lax.psum_scatter(lax.dot_general(tok_rows, flat_weights, (((1,), (1,)), (...  250 us
    all_to_all x1, waiting for transfers between devices, shards(): lax.all_to_all(lax.all_to_all(gate_up, 'wide', split_axis=1, concat_axis=...  93.7 us
    all_to_all x1, blocking collectives, shards(): lax.all_to_all(gate_up, 'wide', split_axis=1, concat_axis=1, tiled=True)  93.4 us
    reduce_scatter x1, waiting for transfers between devices, shards(): return lax.psum_scatter(down_part, 'wide', scatter_dimension=0, tiled=True)  85.8 us
    unnamed x2, other arithmetic  71.5 us
    all_to_all x1, blocking collectives, shards(): lax.all_to_all(down_weight[None], 'wide', split_axis=1, concat_axis=1, ti...  64.5 us
    unnamed x7, local copies, waits for them, and re-layouts  58.8 us
    all_to_all x1, blocking collectives, shards(): lax.all_to_all(lax.all_to_all(down_weight[None], 'wide', split_axis=1, co...  48.4 us
  transfers between devices with their start and end apart: 5, of which 3 were waited for; matrix products, arithmetic and copies ran while one was open for 21% of the time, Pallas kernels for 0%

commit v1 on v0

v1 whole, which is shorter than its diff:
```python
import jax
import jax.numpy as jnp
import numpy as np
from jax import lax
from jax.experimental import pallas as pl
from jax.experimental.pallas import tpu as pltpu
from jax.sharding import PartitionSpec as P

GRID = (2, 4, 2, 2, 4)
RINGS_A = (("z", "y"), ("y", "x"), ("x", "z"))
RINGS_B = (("x", "x"), ("z", "z"), ("y", "y"))
BOTH = ("wide", "narrow")


def partners(rings, flip):
    pairs = []
    for place in np.ndindex(*GRID):
        zh, x, core, zl, y = place
        ring = rings[core]
        if ring == "z":
            z = (2 * zh + zl) ^ flip
            zh, zl = z // 2, z % 2
        elif ring == "x":
            x ^= flip
        elif ring == "y":
            y ^= flip
        else:
            core ^= flip
        pairs.append(
            (
                int(np.ravel_multi_index(place, GRID)),
                int(np.ravel_multi_index((zh, x, core, zl, y), GRID)),
            )
        )
    return pairs


def swap(block, rings, flip):
    return lax.ppermute(block, BOTH, partners(rings, flip))


def gather_direct(block, rings):
    return jnp.stack([block] + [swap(block, rings, flip) for flip in (1, 2, 3)], axis=1)


def gather_relay(block, rings):
    one, three = swap(block, rings, 1), swap(block, rings, 3)
    return block, one, swap(one[0], rings, 3), swap(three[1], rings, 1), three


def column_block(place, step):
    return (place[1] ^ (step // 4)) * 4 + (place[2] ^ (step % 4))


def hidden_kernel(place, *refs):
    parts, (w_own, w_other), (h_own, h_other) = refs[:10], refs[10:12], refs[12:14]
    xa, xb, xk, acc, sems = refs[14:]
    step = pl.program_id(0)
    core = place[0]
    rows_a, rows_b = xa.shape[-2], xb.shape[-2]

    @pl.when(step == 0)
    def _():
        copies = []
        for stream, dest in enumerate((xa, xb)):
            own, one, two_a, two_b, three = parts[5 * stream : 5 * stream + 5]
            pairs = (
                (own, dest.at[0]),
                (one, dest.at[1]),
                (two_a, dest.at[2, 0]),
                (two_b, dest.at[2, 1]),
                (three, dest.at[3]),
            )
            for i, (src, dst) in enumerate(pairs):
                copies.append(pltpu.make_async_copy(src, dst, sems.at[5 * stream + i]))
        for copy in copies:
            copy.start()
        for copy in copies:
            copy.wait()
        acc[...] = jnp.zeros_like(acc)

    zl, y = step // 4, step % 4
    for zh in range(2):
        z = 2 * zh + zl
        for x in range(4):
            for half in range(2):
                row = (zh * 4 + x) * 2 + half
                b = jnp.where(core == 0, x, z)
                d2 = jnp.where(core == 0, y, x)
                d1 = jnp.where(core == 0, z, y)
                xk[pl.ds(row * rows_a, rows_a), :] = xa[b, half, d2 * 4 + d1]
                xk[pl.ds(16 * rows_a + row * rows_b, rows_b), :] = xb[y, half, z * 4 + x]

    total = xk.shape[0]
    chunk = total // 3

    def body(i, carry):
        rows = pl.ds(pl.multiple_of(i * chunk, chunk), chunk)
        lhs = xk[rows, :]
        for part, w in enumerate((w_own, w_other)):
            for which in range(2):
                acc[2 * part + which, rows, :] += lax.dot_general(
                    lhs, w[which], (((1,), (1,)), ((), ())), preferred_element_type=jnp.float32
                )
        return carry

    lax.fori_loop(0, 3, body, 0)

    @pl.when(step == 7)
    def _():
        for part, h in enumerate((h_own, h_other)):
            gate, up = acc[2 * part], acc[2 * part + 1]
            h[...] = (gate / (1 + jnp.exp(-gate)) * up).astype(jnp.bfloat16)


def hidden_call(place, parts, w_own, w_other):
    own_a, own_b = parts[0], parts[5]
    rows_a, rows_b, cols = own_a.shape[-2], own_b.shape[-2], own_a.shape[-1]
    total = 16 * (rows_a + rows_b)
    width = w_own.shape[1]
    w_spec = pl.BlockSpec((2, width, cols), lambda i, p: (0, 0, column_block(p, i)))
    h_spec = pl.BlockSpec((total, width), lambda i, p: (0, 0))
    return pl.pallas_call(
        hidden_kernel,
        out_shape=[jax.ShapeDtypeStruct((total, width), jnp.bfloat16)] * 2,
        grid_spec=pltpu.PrefetchScalarGridSpec(
            num_scalar_prefetch=1,
            grid=(8,),
            in_specs=[pl.BlockSpec(memory_space=pl.ANY)] * 10 + [w_spec, w_spec],
            out_specs=[h_spec, h_spec],
            scratch_shapes=[
                pltpu.VMEM((4, 2, 16, rows_a, cols), jnp.bfloat16),
                pltpu.VMEM((4, 2, 16, rows_b, cols), jnp.bfloat16),
                pltpu.VMEM((total, cols), jnp.bfloat16),
                pltpu.VMEM((4, total, width), jnp.float32),
                pltpu.SemaphoreType.DMA((10,)),
            ],
        ),
        compiler_params=pltpu.CompilerParams(
            dimension_semantics=("arbitrary",), vmem_limit_bytes=48 * 2**20
        ),
        cost_estimate=pl.CostEstimate(
            flops=2 * total * 8 * cols * 4 * width,
            bytes_accessed=2 * 8 * cols * (total + 4 * width),
            transcendentals=2 * total * width,
        ),
    )(place, *parts, w_own, w_other)


def output_kernel(place, h_own, h_other, d_own, d_other, *refs):
    outs, (narrow, wide, sems) = refs[:10], refs[10:]
    step = pl.program_id(0)
    core = place[0]
    slot = step % 2
    total, cols = wide.shape[1], wide.shape[2]
    rows_a, rows_b = outs[0].shape[-2], outs[5].shape[-2]

    def send(stream, b, half, index, row, sem, slot, act):
        rows = rows_b if stream else rows_a
        start = 16 * rows_a + row * rows if stream else row * rows
        own, e1, e3, f1, f3 = outs[5 * stream : 5 * stream + 5]
        src = narrow
        if b == 0:
            dst, src = own.at[half, index], wide
        elif b == 2:
            dst = (e1, e3)[half].at[0, index]
        elif b == 1:
            dst = f1.at[index] if half else e1.at[1, index]
        else:
            dst = e3.at[1, index] if half else f3.at[index]
        act(pltpu.make_async_copy(src.at[slot, pl.ds(start, rows)], dst, sems.at[slot, sem]))

    def move(step, slot, act):
        zl, y = step // 4, step % 4
        for zh in range(2):
            z = 2 * zh + zl
            for x in range(4):
                for half in range(2):
                    row = (zh * 4 + x) * 2 + half

                    @pl.when(core == 0)
                    def _():
                        send(0, x, half, y * 4 + z, row, row, slot, act)

                    for low in range(2):

                        @pl.when((core == 1) & (zl == low))
                        def _():
                            send(0, 2 * zh + low, half, x * 4 + y, row, row, slot, act)

                    for near in range(4):

                        @pl.when(y == near)
                        def _():
                            send(1, near, half, z * 4 + x, row, 16 + row, slot, act)

    @pl.when(step >= 2)
    def _():
        move(step - 2, slot, lambda copy: copy.wait())

    chunk = total // 3

    def body(i, carry):
        rows = pl.ds(pl.multiple_of(i * chunk, chunk), chunk)
        value = jnp.dot(h_own[rows, :], d_own[...], preferred_element_type=jnp.float32)
        value += jnp.dot(h_other[rows, :], d_other[...], preferred_element_type=jnp.float32)
        wide[slot, rows, :] = value
        narrow[slot, rows, :] = value.astype(jnp.bfloat16)
        return carry

    lax.fori_loop(0, 3, body, 0)
    move(step, slot, lambda copy: copy.start())

    @pl.when(step == 7)
    def _():
        move(step - 1, 1 - slot, lambda copy: copy.wait())
        move(step, slot, lambda copy: copy.wait())


def output_call(place, h_own, h_other, d_own, d_other, rows_a, rows_b):
    total, width = h_own.shape
    cols = d_own.shape[1] // 8
    h_spec = pl.BlockSpec((total, width), lambda i, p: (0, 0))
    d_spec = pl.BlockSpec((width, cols), lambda i, p: (0, column_block(p, i)))
    outs = []
    for rows in (rows_a, rows_b):
        outs += [
            jax.ShapeDtypeStruct((2, 16, rows, cols), jnp.float32),
            jax.ShapeDtypeStruct((2, 16, rows, cols), jnp.bfloat16),
            jax.ShapeDtypeStruct((2, 16, rows, cols), jnp.bfloat16),
            jax.ShapeDtypeStruct((16, rows, cols), jnp.bfloat16),
            jax.ShapeDtypeStruct((16, rows, cols), jnp.bfloat16),
        ]
    return pl.pallas_call(
        output_kernel,
        out_shape=outs,
        grid_spec=pltpu.PrefetchScalarGridSpec(
            num_scalar_prefetch=1,
            grid=(8,),
            in_specs=[h_spec, h_spec, d_spec, d_spec],
            out_specs=[pl.BlockSpec(memory_space=pl.ANY)] * 10,
            scratch_shapes=[
                pltpu.VMEM((2, total, cols), jnp.bfloat16),
                pltpu.VMEM((2, total, cols), jnp.float32),
                pltpu.SemaphoreType.DMA((2, 32)),
            ],
        ),
        compiler_params=pltpu.CompilerParams(
            dimension_semantics=("arbitrary",), vmem_limit_bytes=48 * 2**20
        ),
        cost_estimate=pl.CostEstimate(
            flops=2 * total * 8 * cols * 2 * width,
            bytes_accessed=2 * 8 * cols * (total + 2 * width),
            transcendentals=0,
        ),
    )(place, h_own, h_other, d_own, d_other)


def wider(block):
    return block.astype(jnp.float32)


def scatter_relay(blocks, rings):
    own, e1, e3, f1, f3 = blocks
    e1, e3 = swap(e1, rings, 1), swap(e3, rings, 3)
    f3 = swap((wider(f3) + wider(e1[0])).astype(jnp.bfloat16), rings, 3)
    f1 = swap((wider(f1) + wider(e3[0])).astype(jnp.bfloat16), rings, 1)
    return jnp.stack(
        [own[0] + wider(e1[1]) + wider(f3), own[1] + wider(f1) + wider(e3[1])]
    )


def scatter_direct(block, rings, dtype):
    total = block[:, 0]
    for flip in (1, 2, 3):
        total = total + wider(swap(block[:, flip].astype(dtype), rings, flip))
    return total


def shards(tokens, gate_up, down_weight):
    index = lax.axis_index("wide"), lax.axis_index("narrow")
    place = jnp.stack([index[0] % 2, index[1] // 4, index[1] % 4]).astype(jnp.int32)
    rows, cols = tokens.shape
    rows_a, rows_b = rows // 3, rows // 6
    streams = (
        (tokens[: 2 * rows_a].reshape(2, rows_a, cols), RINGS_A),
        (tokens[2 * rows_a :].reshape(2, rows_b, cols), RINGS_B),
    )
    w_other = swap(gate_up, ("core", "core"), 1)
    d_other = swap(down_weight, ("core", "core"), 1)
    firsts = [gather_direct(block, rings[0]) for block, rings in streams]
    seconds = [
        gather_direct(block, rings[1]).reshape(2, 16, block.shape[-2], cols)
        for block, (_, rings) in zip(firsts, streams)
    ]
    parts = [
        part
        for block, (_, rings) in zip(seconds, streams)
        for part in gather_relay(block, rings[2])
    ]
    h_own, h_other = hidden_call(place, parts, gate_up, w_other)
    outs = output_call(place, h_own, h_other, down_weight, d_other, rows_a, rows_b)
    sums = [
        scatter_relay(outs[5 * i : 5 * i + 5], rings[2]).reshape(2, 4, 4, -1, cols)
        for i, (_, rings) in enumerate(streams)
    ]
    sums = [
        scatter_direct(block, rings[1], jnp.bfloat16) for block, (_, rings) in zip(sums, streams)
    ]
    sums = [
        scatter_direct(block, rings[0], jnp.float32) for block, (_, rings) in zip(sums, streams)
    ]
    return jnp.concatenate([block.reshape(-1, cols) for block in sums])


def solution(mesh):
    return jax.shard_map(
        shards,
        mesh=mesh,
        in_specs=(
            P("wide", "narrow"),
            P(None, ("narrow", "wide"), None),
            P(("narrow", "wide"), None),
        ),
        out_specs=P("wide", "narrow"),
        check_vma=False,
    )
```

time: 921 us -> 250 us (0.27)
  waiting for transfers between devices: 430 us -> 141 us
  blocking collectives: 206 us -> 0 us
  local copies, waits for them, and re-layouts: 158 us -> 7.21 us
  other arithmetic: 74.5 us -> 5.55 us
  Pallas kernels: 0 us -> 48.8 us
  starting transfers between devices: 5.11 us -> 47 us
  matrix products: 29.5 us -> 0 us
  between operations: 13.2 us -> 0.33 us
    reduce_scatter x2 -> x0, waiting for transfers between devices: 336 us -> none  [the longest x1 250 us: shards(): lax.psum_scatter(lax.dot_general(tok_rows, flat_weights, (((1,), (1,)), (...]
    all_to_all x3 -> x0, blocking collectives: 206 us -> none  [the longest x1 93.4 us: shards(): lax.all_to_all(gate_up, 'wide', split_axis=1, concat_axis=1, tiled=True)]
    ppermute x0 -> x42, waiting for transfers between devices: none -> 141 us  [swap(): return lax.ppermute(block, BOTH, partners(rings, flip))]
    all_to_all x1 -> x0, waiting for transfers between devices: 93.7 us -> none  [shards(): lax.all_to_all(lax.all_to_all(gate_up, 'wide', split_axis=1, concat_axis=...]
    all_to_all x5 -> x0, local copies, waits for them, and re-layouts: 90.4 us -> none  [the longest x1 28.4 us: shards(): lax.all_to_all(down_weight[None], 'wide', split_axis=1, concat_axis=1, ti...]
    unnamed x2 -> x0, other arithmetic: 71.5 us -> none
    unnamed x7 -> x16, local copies, waits for them, and re-layouts: 58.8 us -> 1.86 us
    pallas_call x0 -> x2, Pallas kernels: none -> 48.8 us  [the longest x1 25.2 us: hidden_call(): pl.pallas_call(hidden_kernel, out_shape=[jax.ShapeDtypeStruct((total, wid...]
  transfers between devices with their start and end apart: 5 -> 42, of which waited for: 3 -> 26; matrix products, arithmetic and copies ran while one was open for 21% -> 4% of each run, Pallas kernels for 0% -> 10%
where the time goes in v1:
time: 250 us
  waiting for transfers between devices  141 us (56%)
  Pallas kernels  48.8 us (20%)
  starting transfers between devices  47 us (19%)
  local copies, waits for them, and re-layouts  7.21 us (3%)
  other arithmetic  5.55 us (2%)
    ppermute x42, waiting for transfers between devices, swap(): return lax.ppermute(block, BOTH, partners(rings, flip))  141 us
    ppermute x42, starting transfers between devices, swap(): return lax.ppermute(block, BOTH, partners(rings, flip))  47 us
    pallas_call x1, Pallas kernels, hidden_call(): pl.pallas_call(hidden_kernel, out_shape=[jax.ShapeDtypeStruct((total, wid...  25.2 us
    pallas_call x1, Pallas kernels, output_call(): pl.pallas_call(output_kernel, out_shape=outs, grid_spec=pltpu.PrefetchSca...  23.6 us
  transfers between devices with their start and end apart: 42, of which 26 were waited for; matrix products, arithmetic and copies ran while one was open for 4% of the time, Pallas kernels for 10%

profile of v1, /device:TPU:1, one launch (start us, length us, event | category | flops | bytes accessed | tf_op | source)
XLA Modules:
  0.0 250.1 jit_solution(627521024975366372)
XLA Ops:
  0.0 1.4 collective-permute-start.20
  1.4 0.9 slice.108
  2.3 2.9 %collective-permute-start.2 = (bf16[2,32,1024]{2,1,0:T(8,128)(2,1)S(1)}, bf16[2,32,1024]{2,1,0:T(8,128)(2,1)S(1)}, u32[]{:S(2)}, u32[]{:S(2)}) collective-permute-start(bf16[2,32,1024]{2,1,0:T(8,128)(2,1)S(1)} %bitcast.200), channel_id=1, source_target_pairs={{0,68},{1,69},{2,70},{3,71},{4,64},{5,65},{6,66},{7,67},{8,11},{9,... | collective-permute-start | bytes 393224 | tf_op jit(solution)/shard_map/ppermute | solution.py:39
  5.2 1.3 collective-permute-start.1
  6.5 1.4 collective-permute-done.2
  7.9 1.2 collective-permute-done
  9.1 1.5 collective-permute-done.1
  10.7 1.3 collective-permute-start.3
  11.9 2.5 collective-permute-start.4
  14.6 0.8 slice.111
  15.4 3.6 %collective-permute-done.3 = bf16[2,4,32,1024]{3,2,1,0:T(8,128)(2,1)S(1)} collective-permute-done((bf16[2,4,32,1024]{3,2,1,0:T(8,128)(2,1)S(1)}, bf16[2,4,32,1024]{3,2,1,0:T(8,128)(2,1)S(1)}, u32[]{:S(2)}, u32[]{:S(2)}) %collective-permute-start.3) | collective-permute-done | bytes 524320 | tf_op jit(solution)/shard_map/ppermute | solution.py:39
  19.1 2.7 %collective-permute-start.11 = (bf16[2,16,1024]{2,1,0:T(8,128)(2,1)S(1)}, bf16[2,16,1024]{2,1,0:T(8,128)(2,1)S(1)}, u32[]{:S(2)}, u32[]{:S(2)}) collective-permute-start(bf16[2,16,1024]{2,1,0:T(8,128)(2,1)S(1)} %bitcast.209), channel_id=1, source_target_pairs={{0,32},{1,33},{2,34},{3,35},{4,36},{5,37},{6,38},{7,39},{8,40},{9,... | collective-permute-start | bytes 196616 | tf_op jit(solution)/shard_map/ppermute | solution.py:39
  21.8 6.3 %collective-permute-done.4 = bf16[2,4,32,1024]{3,2,1,0:T(8,128)(2,1)S(1)} collective-permute-done((bf16[2,4,32,1024]{3,2,1,0:T(8,128)(2,1)S(1)}, bf16[2,4,32,1024]{3,2,1,0:T(8,128)(2,1)S(1)}, u32[]{:S(2)}, u32[]{:S(2)}) %collective-permute-start.4) | collective-permute-done | bytes 524320 | tf_op jit(solution)/shard_map/ppermute | solution.py:39
  28.1 2.8 %collective-permute-done.5 = bf16[2,4,32,1024]{3,2,1,0:T(8,128)(2,1)S(1)} collective-permute-done((bf16[2,4,32,1024]{3,2,1,0:T(8,128)(2,1)S(1)}, bf16[2,4,32,1024]{3,2,1,0:T(8,128)(2,1)S(1)}, u32[]{:S(2)}, u32[]{:S(2)}) %collective-permute-start.5) | collective-permute-done | bytes 524320 | tf_op jit(solution)/shard_map/ppermute | solution.py:39
  31.2 1.7 collective-permute-start.6
  33.0 1.4 collective-permute-start.13
  34.4 3.6 %collective-permute-start.14 = (bf16[2,4,16,1024]{3,2,1,0:T(8,128)(2,1)S(1)}, bf16[2,4,16,1024]{3,2,1,0:T(8,128)(2,1)S(1)}, u32[]{:S(2)}, u32[]{:S(2)}) collective-permute-start(bf16[2,4,16,1024]{3,2,1,0:T(8,128)(2,1)S(1)} %get-tuple-element.48), channel_id=1, source_target_pairs={{0,64},{1,65},{2,66},{3,67},{4,68},{5,69},{6,70},{7,71},{8,72},{9,... | collective-permute-start | bytes 786440 | tf_op jit(solution)/shard_map/ppermute | solution.py:39
  38.0 27.1 %collective-permute-done.13 = bf16[2,4,16,1024]{3,2,1,0:T(8,128)(2,1)S(1)} collective-permute-done((bf16[2,4,16,1024]{3,2,1,0:T(8,128)(2,1)S(1)}, bf16[2,4,16,1024]{3,2,1,0:T(8,128)(2,1)S(1)}, u32[]{:S(2)}, u32[]{:S(2)}) %collective-permute-start.13) | collective-permute-done | bytes 262176 | tf_op jit(solution)/shard_map/ppermute | solution.py:39
  65.1 3.9 %collective-permute-start.8 = (bf16[2,16,32,1024]{3,2,1,0:T(8,128)(2,1)S(1)}, bf16[2,16,32,1024]{3,2,1,0:T(8,128)(2,1)S(1)}, u32[]{:S(2)}, u32[]{:S(2)}) collective-permute-start(bf16[2,16,32,1024]{3,2,1,0:T(8,128)(2,1)S(1)} %bitcast.197), channel_id=1, source_target_pairs={{0,48},{1,49},{2,50},{3,51},{4,52},{5,53},{6,54},{7,55},{8,76},{9,... | collective-permute-start | bytes 6291464 | tf_op jit(solution)/shard_map/ppermute | solution.py:39
  69.0 2.3 collective-permute-done.14
  71.4 1.2 collective-permute-start.16
  72.7 12.8 %collective-permute-done.16.refs_6_ = bf16[2,16,16,1024]{3,2,1,0:T(8,128)(2,1)S(1)} collective-permute-done((bf16[2,16,16,1024]{3,2,1,0:T(8,128)(2,1)S(1)}, bf16[2,16,16,1024]{3,2,1,0:T(8,128)(2,1)S(1)}, u32[]{:S(2)}, u32[]{:S(2)}) %collective-permute-start.16) | collective-permute-done | bytes 1048608 | tf_op jit(solution)/shard_map/ppermute | solution.py:39
  85.5 2.4 collective-permute-start.18
  87.9 0.4 collective-permute-start.17
  88.3 1.2 slice_bitcast_fusion.4
  89.5 4.4 %collective-permute-done.8.refs_4_ = bf16[2,16,32,1024]{3,2,1,0:T(8,128)(2,1)S(1)} collective-permute-done((bf16[2,16,32,1024]{3,2,1,0:T(8,128)(2,1)S(1)}, bf16[2,16,32,1024]{3,2,1,0:T(8,128)(2,1)S(1)}, u32[]{:S(2)}, u32[]{:S(2)}) %collective-permute-start.8) | collective-permute-done | bytes 2097184 | tf_op jit(solution)/shard_map/ppermute | solution.py:39
  94.0 1.4 collective-permute-start.7
  95.4 1.1 slice_bitcast_fusion.3
  96.5 8.9 %collective-permute-done.18.refs_9_ = bf16[2,16,16,1024]{3,2,1,0:T(8,128)(2,1)S(1)} collective-permute-done((bf16[2,16,16,1024]{3,2,1,0:T(8,128)(2,1)S(1)}, bf16[2,16,16,1024]{3,2,1,0:T(8,128)(2,1)S(1)}, u32[]{:S(2)}, u32[]{:S(2)}) %collective-permute-start.18) | collective-permute-done | bytes 1048608 | tf_op jit(solution)/shard_map/ppermute | solution.py:39
  105.4 0.9 slice_bitcast_fusion.11
  106.3 4.7 %collective-permute-done.17.refs_7_ = bf16[16,16,1024]{2,1,0:T(8,128)(2,1)S(1)} collective-permute-done((bf16[16,16,1024]{2,1,0:T(8,128)(2,1)S(1)}, bf16[16,16,1024]{2,1,0:T(8,128)(2,1)S(1)}, u32[]{:S(2)}, u32[]{:S(2)}) %collective-permute-start.17) | collective-permute-done | bytes 524320 | tf_op jit(solution)/shard_map/ppermute | solution.py:39
  111.0 0.8 copy-done
  111.9 8.3 %collective-permute-done.19.refs_8_ = bf16[16,16,1024]{2,1,0:T(8,128)(2,1)} collective-permute-done((bf16[16,16,1024]{2,1,0:T(8,128)(2,1)}, bf16[16,16,1024]{2,1,0:T(8,128)(2,1)}, u32[]{:S(2)}, u32[]{:S(2)}) %collective-permute-start.19) | collective-permute-done | bytes 524320 | tf_op jit(solution)/shard_map/ppermute | solution.py:39
  120.2 1.0 copy-done.1
  121.2 25.2 %shard_map.37 = (bf16[768,224]{1,0:T(8,128)(2,1)S(1)}, bf16[768,224]{1,0:T(8,128)(2,1)S(1)}) custom-call(s32[3]{0:T(128)S(1)} %pad_add_fusion.place, bf16[2,16,32,1024]{3,2,1,0:T(8,128)(2,1)} %bitcast.198, bf16[2,16,32,1024]{3,2,1,0:T(8,128)(2,1)} %copy-done.5, bf16[16,32,1024]{2,1,0:T(8,128)(2,1)S(1)} %collective-permute-done.7.refs_2_, ...), custom_call_target="tpu_custom_call" | custom-call | flops 11274289152 | bytes 27262976 | tf_op jit(solution)/shard_map/pallas_call | solution.py:123
  146.4 23.6 %shard_map.38 = (f32[2,16,32,1024]{3,2,1,0:T(8,128)}, bf16[2,16,32,1024]{3,2,1,0:T(8,128)(2,1)}, bf16[2,16,32,1024]{3,2,1,0:T(8,128)(2,1)}, bf16[16,32,1024]{2,1...) custom-call(s32[3]{0:T(128)S(1)} %pad_add_fusion.place, ...), custom_call_target="tpu_custom_call" | custom-call | flops 5637144576 | bytes 19922944 | tf_op jit(solution)/shard_map/pallas_call | solution.py:234
  170.3 1.4 collective-permute-start.34
  171.7 18.6 %collective-permute-done.32 = bf16[2,16,16,1024]{3,2,1,0:T(8,128)(2,1)S(1)} collective-permute-done((bf16[2,16,16,1024]{3,2,1,0:T(8,128)(2,1)S(1)}, bf16[2,16,16,1024]{3,2,1,0:T(8,128)(2,1)S(1)}, u32[]{:S(2)}, u32[]{:S(2)}) %collective-permute-start.32) | collective-permute-done | bytes 1048608 | tf_op jit(solution)/shard_map/ppermute | solution.py:39
  190.6 2.2 collective-permute-done.34
  193.0 1.0 collective-permute-start.35
  194.0 1.4 collective-permute-done.22
  195.5 0.4 fusion.3
  196.0 0.8 collective-permute-done.24
  196.8 0.4 fusion.2
  197.4 2.7 %collective-permute-done.33 = bf16[16,16,1024]{2,1,0:T(8,128)(2,1)S(1)} collective-permute-done((bf16[16,16,1024]{2,1,0:T(8,128)(2,1)S(1)}, bf16[16,16,1024]{2,1,0:T(8,128)(2,1)S(1)}, u32[]{:S(2)}, u32[]{:S(2)}) %collective-permute-start.33) | collective-permute-done | bytes 524320 | tf_op jit(solution)/shard_map/ppermute | solution.py:39
  200.1 1.5 collective-permute-done.35
  201.6 0.6 convert_add_fusion.3
  202.5 2.0 collective-permute-start.37
  204.6 1.8 collective-permute-start.38
  206.4 9.6 %collective-permute-done.23 = bf16[16,32,1024]{2,1,0:T(8,128)(2,1)S(1)} collective-permute-done((bf16[16,32,1024]{2,1,0:T(8,128)(2,1)S(1)}, bf16[16,32,1024]{2,1,0:T(8,128)(2,1)S(1)}, u32[]{:S(2)}, u32[]{:S(2)}) %collective-permute-start.23) | collective-permute-done | bytes 1048608 | tf_op jit(solution)/shard_map/ppermute | solution.py:39
  216.0 1.3 convert_add_fusion
  217.9 2.5 collective-permute-start.27
  220.4 1.4 collective-permute-start.28
  222.0 2.5 collective-permute-start.40
  224.5 1.4 collective-permute-done.26
  225.9 1.3 collective-permute-start.41
  227.2 5.4 %collective-permute-done.27 = bf16[2,4,32,1024]{3,2,1,0:T(8,128)(2,1)S(1)} collective-permute-done((bf16[2,4,32,1024]{3,2,1,0:T(8,128)(2,1)S(1)}, bf16[2,4,32,1024]{3,2,1,0:T(8,128)(2,1)S(1)}, u32[]{:S(2)}, u32[]{:S(2)}) %collective-permute-start.27) | collective-permute-done | bytes 524320 | tf_op jit(solution)/shard_map/ppermute | solution.py:39
  232.7 4.0 %collective-permute-done.28 = bf16[2,4,32,1024]{3,2,1,0:T(8,128)(2,1)S(1)} collective-permute-done((bf16[2,4,32,1024]{3,2,1,0:T(8,128)(2,1)S(1)}, bf16[2,4,32,1024]{3,2,1,0:T(8,128)(2,1)S(1)}, u32[]{:S(2)}, u32[]{:S(2)}) %collective-permute-start.28) | collective-permute-done | bytes 524320 | tf_op jit(solution)/shard_map/ppermute | solution.py:39
  237.1 2.8 %collective-permute-start.30 = (f32[2,32,1024]{2,1,0:T(8,128)S(1)}, f32[2,32,1024]{2,1,0:T(8,128)S(1)}, u32[]{:S(2)}, u32[]{:S(2)}) collective-permute-start(f32[2,32,1024]{2,1,0:T(8,128)S(1)} %get-tuple-element.38), channel_id=1, source_target_pairs={{0,64},{1,65},{2,66},{3,67},{4,68},{5,69},{6,70},{7,71},{8,10},{9,... | collective-permute-start | bytes 786440 | tf_op jit(solution)/shard_map/ppermute | solution.py:39
  240.0 1.0 collective-permute-start.31
  241.0 1.3 collective-permute-done.29
  242.3 4.3 %collective-permute-done.30 = f32[2,32,1024]{2,1,0:T(8,128)S(1)} collective-permute-done((f32[2,32,1024]{2,1,0:T(8,128)S(1)}, f32[2,32,1024]{2,1,0:T(8,128)S(1)}, u32[]{:S(2)}, u32[]{:S(2)}) %collective-permute-start.30) | collective-permute-done | bytes 262176 | tf_op jit(solution)/shard_map/ppermute | solution.py:39
  246.6 2.6 %collective-permute-done.31 = f32[2,32,1024]{2,1,0:T(8,128)S(1)} collective-permute-done((f32[2,32,1024]{2,1,0:T(8,128)S(1)}, f32[2,32,1024]{2,1,0:T(8,128)S(1)}, u32[]{:S(2)}, u32[]{:S(2)}) %collective-permute-start.31) | collective-permute-done | bytes 262176 | tf_op jit(solution)/shard_map/ppermute | solution.py:39
  249.3 0.8 pad_maximum_fusion.5
  (66 shorter events, 3.7 us)
Async XLA Ops:
  0.0 120.2 %collective-permute-start.20 = (bf16[2,224,8192]{2,1,0:T(8,128)(2,1)}, bf16[2,224,8192]{2,1,0:T(8,128)(2,1)}, u32[]{:S(2)}, u32[]{:S(2)}) collective-permute-start(bf16[2,224,8192]{2,1,0:T(8,128)(2,1)} %refs_10_.1), channel_id=1, source_target_pairs={{0,8},{1,9},{2,10},{3,11},{4,12},{5,13},{6,14},{7,15},{8,0},{9,1},... | collective-permute-start | bytes 22020104 | tf_op jit(solution)/shard_map/ppermute | solution.py:39
  2.3 5.6 %collective-permute-start.2 = (bf16[2,32,1024]{2,1,0:T(8,128)(2,1)S(1)}, bf16[2,32,1024]{2,1,0:T(8,128)(2,1)S(1)}, u32[]{:S(2)}, u32[]{:S(2)}) collective-permute-start(bf16[2,32,1024]{2,1,0:T(8,128)(2,1)S(1)} %bitcast.200), channel_id=1, source_target_pairs={{0,68},{1,69},{2,70},{3,71},{4,64},{5,65},{6,66},{7,67},{8,11},{9,... | collective-permute-start | bytes 393224 | tf_op jit(solution)/shard_map/ppermute | solution.py:39
  5.2 3.9 %collective-permute-start = (bf16[2,32,1024]{2,1,0:T(8,128)(2,1)S(1)}, bf16[2,32,1024]{2,1,0:T(8,128)(2,1)S(1)}, u32[]{:S(2)}, u32[]{:S(2)}) collective-permute-start(bf16[2,32,1024]{2,1,0:T(8,128)(2,1)S(1)} %bitcast.201), channel_id=1, source_target_pairs={{0,4},{1,5},{2,6},{3,7},{4,0},{5,1},{6,2},{7,3},{8,9},{9,8},{10,11... | collective-permute-start | bytes 393224 | tf_op jit(solution)/shard_map/ppermute | solution.py:39
  5.2 5.3 %collective-permute-start.1 = (bf16[2,32,1024]{2,1,0:T(8,128)(2,1)S(1)}, bf16[2,32,1024]{2,1,0:T(8,128)(2,1)S(1)}, u32[]{:S(2)}, u32[]{:S(2)}) collective-permute-start(bf16[2,32,1024]{2,1,0:T(8,128)(2,1)S(1)} %bitcast.202), channel_id=1, source_target_pairs={{0,64},{1,65},{2,66},{3,67},{4,68},{5,69},{6,70},{7,71},{8,10},{9,... | collective-permute-start | bytes 393224 | tf_op jit(solution)/shard_map/ppermute | solution.py:39
  10.7 8.4 %collective-permute-start.3 = (bf16[2,4,32,1024]{3,2,1,0:T(8,128)(2,1)S(1)}, bf16[2,4,32,1024]{3,2,1,0:T(8,128)(2,1)S(1)}, u32[]{:S(2)}, u32[]{:S(2)}) collective-permute-start(bf16[2,4,32,1024]{3,2,1,0:T(8,128)(2,1)S(1)} %get-tuple-element.46), channel_id=1, source_target_pairs={{0,1},{1,0},{2,3},{3,2},{4,5},{5,4},{6,7},{7,6},{8,24},{9,25},{10,... | collective-permute-start | bytes 1572872 | tf_op jit(solution)/shard_map/ppermute | solution.py:39
  11.9 16.2 %collective-permute-start.4 = (bf16[2,4,32,1024]{3,2,1,0:T(8,128)(2,1)S(1)}, bf16[2,4,32,1024]{3,2,1,0:T(8,128)(2,1)S(1)}, u32[]{:S(2)}, u32[]{:S(2)}) collective-permute-start(bf16[2,4,32,1024]{3,2,1,0:T(8,128)(2,1)S(1)} %get-tuple-element.46), channel_id=1, source_target_pairs={{0,2},{1,3},{2,0},{3,1},{4,6},{5,7},{6,4},{7,5},{8,40},{9,41},{10,... | collective-permute-start | bytes 1572872 | tf_op jit(solution)/shard_map/ppermute | solution.py:39
  14.4 16.6 %collective-permute-start.5 = (bf16[2,4,32,1024]{3,2,1,0:T(8,128)(2,1)S(1)}, bf16[2,4,32,1024]{3,2,1,0:T(8,128)(2,1)S(1)}, u32[]{:S(2)}, u32[]{:S(2)}) collective-permute-start(bf16[2,4,32,1024]{3,2,1,0:T(8,128)(2,1)S(1)} %get-tuple-element.46), channel_id=1, source_target_pairs={{0,3},{1,2},{2,1},{3,0},{4,7},{5,6},{6,5},{7,4},{8,56},{9,57},{10,... | collective-permute-start | bytes 1572872 | tf_op jit(solution)/shard_map/ppermute | solution.py:39
  15.4 17.5 %collective-permute-start.10 = (bf16[2,16,1024]{2,1,0:T(8,128)(2,1)S(1)}, bf16[2,16,1024]{2,1,0:T(8,128)(2,1)S(1)}, u32[]{:S(2)}, u32[]{:S(2)}) collective-permute-start(bf16[2,16,1024]{2,1,0:T(8,128)(2,1)S(1)} %bitcast.208), channel_id=1, source_target_pairs={{0,16},{1,17},{2,18},{3,19},{4,20},{5,21},{6,22},{7,23},{8,24},{9,... | collective-permute-start | bytes 196616 | tf_op jit(solution)/shard_map/ppermute | solution.py:39
  19.1 13.9 %collective-permute-start.11 = (bf16[2,16,1024]{2,1,0:T(8,128)(2,1)S(1)}, bf16[2,16,1024]{2,1,0:T(8,128)(2,1)S(1)}, u32[]{:S(2)}, u32[]{:S(2)}) collective-permute-start(bf16[2,16,1024]{2,1,0:T(8,128)(2,1)S(1)} %bitcast.209), channel_id=1, source_target_pairs={{0,32},{1,33},{2,34},{3,35},{4,36},{5,37},{6,38},{7,39},{8,40},{9,... | collective-permute-start | bytes 196616 | tf_op jit(solution)/shard_map/ppermute | solution.py:39
  28.1 4.8 %collective-permute-start.12 = (bf16[2,16,1024]{2,1,0:T(8,128)(2,1)S(1)}, bf16[2,16,1024]{2,1,0:T(8,128)(2,1)S(1)}, u32[]{:S(2)}, u32[]{:S(2)}) collective-permute-start(bf16[2,16,1024]{2,1,0:T(8,128)(2,1)S(1)} %bitcast.210), channel_id=1, source_target_pairs={{0,48},{1,49},{2,50},{3,51},{4,52},{5,53},{6,54},{7,55},{8,56},{9,... | collective-permute-start | bytes 196616 | tf_op jit(solution)/shard_map/ppermute | solution.py:39
  31.2 58.3 %copy-start.4 = (bf16[2,4,4,32,1024]{4,3,2,1,0:T(8,128)(2,1)}, bf16[2,4,4,32,1024]{4,3,2,1,0:T(8,128)(2,1)S(1)}, u32[]{:S(2)}) copy-start(bf16[2,4,4,32,1024]{4,3,2,1,0:T(8,128)(2,1)S(1)} %pad_maximum_fusion.2) | copy-start | bytes 6291460
  31.2 56.6 %collective-permute-start.6 = (bf16[2,16,32,1024]{3,2,1,0:T(8,128)(2,1)S(1)}, bf16[2,16,32,1024]{3,2,1,0:T(8,128)(2,1)S(1)}, u32[]{:S(2)}, u32[]{:S(2)}) collective-permute-start(bf16[2,16,32,1024]{3,2,1,0:T(8,128)(2,1)S(1)} %bitcast.196), channel_id=1, source_target_pairs={{0,16},{1,17},{2,18},{3,19},{4,20},{5,21},{6,22},{7,23},{8,12},{9,... | collective-permute-start | bytes 6291464 | tf_op jit(solution)/shard_map/ppermute | solution.py:39
  33.0 32.1 %collective-permute-start.13 = (bf16[2,4,16,1024]{3,2,1,0:T(8,128)(2,1)S(1)}, bf16[2,4,16,1024]{3,2,1,0:T(8,128)(2,1)S(1)}, u32[]{:S(2)}, u32[]{:S(2)}) collective-permute-start(bf16[2,4,16,1024]{3,2,1,0:T(8,128)(2,1)S(1)} %get-tuple-element.48), channel_id=1, source_target_pairs={{0,4},{1,5},{2,6},{3,7},{4,0},{5,1},{6,2},{7,3},{8,12},{9,13},{10,... | collective-permute-start | bytes 786440 | tf_op jit(solution)/shard_map/ppermute | solution.py:39
  34.4 36.9 %collective-permute-start.14 = (bf16[2,4,16,1024]{3,2,1,0:T(8,128)(2,1)S(1)}, bf16[2,4,16,1024]{3,2,1,0:T(8,128)(2,1)S(1)}, u32[]{:S(2)}, u32[]{:S(2)}) collective-permute-start(bf16[2,4,16,1024]{3,2,1,0:T(8,128)(2,1)S(1)} %get-tuple-element.48), channel_id=1, source_target_pairs={{0,64},{1,65},{2,66},{3,67},{4,68},{5,69},{6,70},{7,71},{8,72},{9,... | collective-permute-start | bytes 786440 | tf_op jit(solution)/shard_map/ppermute | solution.py:39
  38.0 33.3 %collective-permute-start.15 = (bf16[2,4,16,1024]{3,2,1,0:T(8,128)(2,1)S(1)}, bf16[2,4,16,1024]{3,2,1,0:T(8,128)(2,1)S(1)}, u32[]{:S(2)}, u32[]{:S(2)}) collective-permute-start(bf16[2,4,16,1024]{3,2,1,0:T(8,128)(2,1)S(1)} %get-tuple-element.48), channel_id=1, source_target_pairs={{0,68},{1,69},{2,70},{3,71},{4,64},{5,65},{6,66},{7,67},{8,76},{9,... | collective-permute-start | bytes 786440 | tf_op jit(solution)/shard_map/ppermute | solution.py:39
  65.1 28.9 %collective-permute-start.8 = (bf16[2,16,32,1024]{3,2,1,0:T(8,128)(2,1)S(1)}, bf16[2,16,32,1024]{3,2,1,0:T(8,128)(2,1)S(1)}, u32[]{:S(2)}, u32[]{:S(2)}) collective-permute-start(bf16[2,16,32,1024]{3,2,1,0:T(8,128)(2,1)S(1)} %bitcast.197), channel_id=1, source_target_pairs={{0,48},{1,49},{2,50},{3,51},{4,52},{5,53},{6,54},{7,55},{8,76},{9,... | collective-permute-start | bytes 6291464 | tf_op jit(solution)/shard_map/ppermute | solution.py:39
  71.4 14.0 %collective-permute-start.16 = (bf16[2,16,16,1024]{3,2,1,0:T(8,128)(2,1)S(1)}, bf16[2,16,16,1024]{3,2,1,0:T(8,128)(2,1)S(1)}, u32[]{:S(2)}, u32[]{:S(2)}) collective-permute-start(bf16[2,16,16,1024]{3,2,1,0:T(8,128)(2,1)S(1)} %bitcast.185), channel_id=1, source_target_pairs={{0,1},{1,0},{2,3},{3,2},{4,5},{5,4},{6,7},{7,6},{8,9},{9,8},{10,11... | collective-permute-start | bytes 3145736 | tf_op jit(solution)/shard_map/ppermute | solution.py:39
  72.7 73.7 %collective-permute-start.21 = (bf16[224,8192]{1,0:T(8,128)(2,1)}, bf16[224,8192]{1,0:T(8,128)(2,1)}, u32[]{:S(2)}, u32[]{:S(2)}) collective-permute-start(bf16[224,8192]{1,0:T(8,128)(2,1)} %d_own.1), channel_id=1, source_target_pairs={{0,8},{1,9},{2,10},{3,11},{4,12},{5,13},{6,14},{7,15},{8,0},{9,1},... | collective-permute-start | bytes 11010056 | tf_op jit(solution)/shard_map/ppermute | solution.py:39
  85.5 19.9 %collective-permute-start.18 = (bf16[2,16,16,1024]{3,2,1,0:T(8,128)(2,1)S(1)}, bf16[2,16,16,1024]{3,2,1,0:T(8,128)(2,1)S(1)}, u32[]{:S(2)}, u32[]{:S(2)}) collective-permute-start(bf16[2,16,16,1024]{3,2,1,0:T(8,128)(2,1)S(1)} %bitcast.186), channel_id=1, source_target_pairs={{0,3},{1,2},{2,1},{3,0},{4,7},{5,6},{6,5},{7,4},{8,11},{9,10},{10,... | collective-permute-start | bytes 3145736 | tf_op jit(solution)/shard_map/ppermute | solution.py:39
  87.9 8.6 %copy-start.5 = (bf16[2,16,32,1024]{3,2,1,0:T(8,128)(2,1)}, bf16[2,16,32,1024]{3,2,1,0:T(8,128)(2,1)S(1)}, u32[]{:S(2)}) copy-start(bf16[2,16,32,1024]{3,2,1,0:T(8,128)(2,1)S(1)} %collective-permute-done.6.refs_1_) | copy-start | bytes 6291460
  87.9 23.1 %collective-permute-start.17 = (bf16[16,16,1024]{2,1,0:T(8,128)(2,1)S(1)}, bf16[16,16,1024]{2,1,0:T(8,128)(2,1)S(1)}, u32[]{:S(2)}, u32[]{:S(2)}) collective-permute-start(bf16[16,16,1024]{2,1,0:T(8,128)(2,1)S(1)} %slice_bitcast_fusion.12), channel_id=1, source_target_pairs={{0,3},{1,2},{2,1},{3,0},{4,7},{5,6},{6,5},{7,4},{8,11},{9,10},{10,... | collective-permute-start | bytes 1572872 | tf_op jit(solution)/shard_map/ppermute | solution.py:39
  94.0 17.0 %copy-start.6 = (bf16[2,16,32,1024]{3,2,1,0:T(8,128)(2,1)}, bf16[2,16,32,1024]{3,2,1,0:T(8,128)(2,1)S(1)}, u32[]{:S(2)}) copy-start(bf16[2,16,32,1024]{3,2,1,0:T(8,128)(2,1)S(1)} %collective-permute-done.8.refs_4_) | copy-start | bytes 6291460
  94.0 26.2 %collective-permute-start.7 = (bf16[16,32,1024]{2,1,0:T(8,128)(2,1)}, bf16[16,32,1024]{2,1,0:T(8,128)(2,1)S(1)}, u32[]{:S(2)}, u32[]{:S(2)}) collective-permute-start(bf16[16,32,1024]{2,1,0:T(8,128)(2,1)} %slice_bitcast_fusion.4), channel_id=1, source_target_pairs={{0,48},{1,49},{2,50},{3,51},{4,52},{5,53},{6,54},{7,55},{8,76},{9,... | collective-permute-start | bytes 3145736 | tf_op jit(solution)/shard_map/ppermute | solution.py:39
  105.4 6.4 %copy-start.7 = (bf16[2,16,16,1024]{3,2,1,0:T(8,128)(2,1)}, bf16[2,16,16,1024]{3,2,1,0:T(8,128)(2,1)S(1)}, u32[]{:S(2)}) copy-start(bf16[2,16,16,1024]{3,2,1,0:T(8,128)(2,1)S(1)} %collective-permute-done.18.refs_9_) | copy-start | bytes 3145732
  105.4 14.8 %collective-permute-start.9 = (bf16[16,32,1024]{2,1,0:T(8,128)(2,1)}, bf16[16,32,1024]{2,1,0:T(8,128)(2,1)}, u32[]{:S(2)}, u32[]{:S(2)}) collective-permute-start(bf16[16,32,1024]{2,1,0:T(8,128)(2,1)} %slice_bitcast_fusion.3), channel_id=1, source_target_pairs={{0,16},{1,17},{2,18},{3,19},{4,20},{5,21},{6,22},{7,23},{8,12},{9,... | collective-permute-start | bytes 3145736 | tf_op jit(solution)/shard_map/ppermute | solution.py:39
  111.0 0.8 copy-start
  111.8 8.3 %collective-permute-start.19 = (bf16[16,16,1024]{2,1,0:T(8,128)(2,1)}, bf16[16,16,1024]{2,1,0:T(8,128)(2,1)}, u32[]{:S(2)}, u32[]{:S(2)}) collective-permute-start(bf16[16,16,1024]{2,1,0:T(8,128)(2,1)} %slice_bitcast_fusion.11), channel_id=1, source_target_pairs={{0,1},{1,0},{2,3},{3,2},{4,5},{5,4},{6,7},{7,6},{8,9},{9,8},{10,11... | collective-permute-start | bytes 1572872 | tf_op jit(solution)/shard_map/ppermute | solution.py:39
  120.2 1.0 copy-start.1
  170.0 25.5 %collective-permute-start.22 = (bf16[2,16,32,1024]{3,2,1,0:T(8,128)(2,1)}, bf16[2,16,32,1024]{3,2,1,0:T(8,128)(2,1)S(1)}, u32[]{:S(2)}, u32[]{:S(2)}) collective-permute-start(bf16[2,16,32,1024]{3,2,1,0:T(8,128)(2,1)} %get-tuple-element.20), channel_id=1, source_target_pairs={{0,16},{1,17},{2,18},{3,19},{4,20},{5,21},{6,22},{7,23},{8,12},{9,... | collective-permute-start | bytes 6291464 | tf_op jit(solution)/shard_map/ppermute | solution.py:39
  170.1 26.7 %collective-permute-start.24 = (bf16[2,16,32,1024]{3,2,1,0:T(8,128)(2,1)}, bf16[2,16,32,1024]{3,2,1,0:T(8,128)(2,1)S(1)}, u32[]{:S(2)}, u32[]{:S(2)}) collective-permute-start(bf16[2,16,32,1024]{3,2,1,0:T(8,128)(2,1)} %get-tuple-element.23), channel_id=1, source_target_pairs={{0,48},{1,49},{2,50},{3,51},{4,52},{5,53},{6,54},{7,55},{8,76},{9,... | collective-permute-start | bytes 6291464 | tf_op jit(solution)/shard_map/ppermute | solution.py:39
  170.2 20.1 %collective-permute-start.32 = (bf16[2,16,16,1024]{3,2,1,0:T(8,128)(2,1)S(1)}, bf16[2,16,16,1024]{3,2,1,0:T(8,128)(2,1)S(1)}, u32[]{:S(2)}, u32[]{:S(2)}) collective-permute-start(bf16[2,16,16,1024]{3,2,1,0:T(8,128)(2,1)S(1)} %get-tuple-element.25), channel_id=1, source_target_pairs={{0,1},{1,0},{2,3},{3,2},{4,5},{5,4},{6,7},{7,6},{8,9},{9,8},{10,11... | collective-permute-start | bytes 3145736 | tf_op jit(solution)/shard_map/ppermute | solution.py:39
  170.3 22.5 %collective-permute-start.34 = (bf16[2,16,16,1024]{3,2,1,0:T(8,128)(2,1)S(1)}, bf16[2,16,16,1024]{3,2,1,0:T(8,128)(2,1)S(1)}, u32[]{:S(2)}, u32[]{:S(2)}) collective-permute-start(bf16[2,16,16,1024]{3,2,1,0:T(8,128)(2,1)S(1)} %get-tuple-element.28), channel_id=1, source_target_pairs={{0,3},{1,2},{2,1},{3,0},{4,7},{5,6},{6,5},{7,4},{8,11},{9,10},{10,... | collective-permute-start | bytes 3145736 | tf_op jit(solution)/shard_map/ppermute | solution.py:39
  190.5 9.6 %collective-permute-start.33 = (bf16[16,16,1024]{2,1,0:T(8,128)(2,1)S(1)}, bf16[16,16,1024]{2,1,0:T(8,128)(2,1)S(1)}, u32[]{:S(2)}, u32[]{:S(2)}) collective-permute-start(bf16[16,16,1024]{2,1,0:T(8,128)(2,1)S(1)} %fusion.10), channel_id=1, source_target_pairs={{0,3},{1,2},{2,1},{3,0},{4,7},{5,6},{6,5},{7,4},{8,11},{9,10},{10,... | collective-permute-start | bytes 1572872 | tf_op jit(solution)/shard_map/ppermute | solution.py:39
  193.0 8.6 %collective-permute-start.35 = (bf16[16,16,1024]{2,1,0:T(8,128)(2,1)S(1)}, bf16[16,16,1024]{2,1,0:T(8,128)(2,1)S(1)}, u32[]{:S(2)}, u32[]{:S(2)}) collective-permute-start(bf16[16,16,1024]{2,1,0:T(8,128)(2,1)S(1)} %fusion.9), channel_id=1, source_target_pairs={{0,1},{1,0},{2,3},{3,2},{4,5},{5,4},{6,7},{7,6},{8,9},{9,8},{10,11... | collective-permute-start | bytes 1572872 | tf_op jit(solution)/shard_map/ppermute | solution.py:39
  195.9 5.7 %copy-start.3 = (f32[2,16,16,1024]{3,2,1,0:T(8,128)S(1)}, f32[2,16,16,1024]{3,2,1,0:T(8,128)}, u32[]{:S(2)}) copy-start(f32[2,16,16,1024]{3,2,1,0:T(8,128)} %get-tuple-element.24) | copy-start | bytes 6291460
  195.9 20.1 %collective-permute-start.23 = (bf16[16,32,1024]{2,1,0:T(8,128)(2,1)S(1)}, bf16[16,32,1024]{2,1,0:T(8,128)(2,1)S(1)}, u32[]{:S(2)}, u32[]{:S(2)}) collective-permute-start(bf16[16,32,1024]{2,1,0:T(8,128)(2,1)S(1)} %fusion.3), channel_id=1, source_target_pairs={{0,48},{1,49},{2,50},{3,51},{4,52},{5,53},{6,54},{7,55},{8,76},{9,... | collective-permute-start | bytes 3145736 | tf_op jit(solution)/shard_map/ppermute | solution.py:39
  197.2 18.8 %collective-permute-start.25 = (bf16[16,32,1024]{2,1,0:T(8,128)(2,1)S(1)}, bf16[16,32,1024]{2,1,0:T(8,128)(2,1)S(1)}, u32[]{:S(2)}, u32[]{:S(2)}) collective-permute-start(bf16[16,32,1024]{2,1,0:T(8,128)(2,1)S(1)} %fusion.2), channel_id=1, source_target_pairs={{0,16},{1,17},{2,18},{3,19},{4,20},{5,21},{6,22},{7,23},{8,12},{9,... | collective-permute-start | bytes 3145736 | tf_op jit(solution)/shard_map/ppermute | solution.py:39
  202.2 13.8 %copy-start.2 = (f32[2,16,32,1024]{3,2,1,0:T(8,128)S(1)}, f32[2,16,32,1024]{3,2,1,0:T(8,128)}, u32[]{:S(2)}) copy-start(f32[2,16,32,1024]{3,2,1,0:T(8,128)} %get-tuple-element.19) | copy-start | bytes 12582916
  202.4 17.9 %collective-permute-start.36 = (bf16[2,4,16,1024]{3,2,1,0:T(8,128)(2,1)S(1)}, bf16[2,4,16,1024]{3,2,1,0:T(8,128)(2,1)S(1)}, u32[]{:S(2)}, u32[]{:S(2)}) collective-permute-start(bf16[2,4,16,1024]{3,2,1,0:T(8,128)(2,1)S(1)} %get-tuple-element.39), channel_id=1, source_target_pairs={{0,4},{1,5},{2,6},{3,7},{4,0},{5,1},{6,2},{7,3},{8,12},{9,13},{10,... | collective-permute-start | bytes 786440 | tf_op jit(solution)/shard_map/ppermute | solution.py:39
  202.5 19.2 %collective-permute-start.37 = (bf16[2,4,16,1024]{3,2,1,0:T(8,128)(2,1)S(1)}, bf16[2,4,16,1024]{3,2,1,0:T(8,128)(2,1)S(1)}, u32[]{:S(2)}, u32[]{:S(2)}) collective-permute-start(bf16[2,4,16,1024]{3,2,1,0:T(8,128)(2,1)S(1)} %get-tuple-element.41), channel_id=1, source_target_pairs={{0,64},{1,65},{2,66},{3,67},{4,68},{5,69},{6,70},{7,71},{8,72},{9,... | collective-permute-start | bytes 786440 | tf_op jit(solution)/shard_map/ppermute | solution.py:39
  204.6 17.2 %collective-permute-start.38 = (bf16[2,4,16,1024]{3,2,1,0:T(8,128)(2,1)S(1)}, bf16[2,4,16,1024]{3,2,1,0:T(8,128)(2,1)S(1)}, u32[]{:S(2)}, u32[]{:S(2)}) collective-permute-start(bf16[2,4,16,1024]{3,2,1,0:T(8,128)(2,1)S(1)} %get-tuple-element.40), channel_id=1, source_target_pairs={{0,68},{1,69},{2,70},{3,71},{4,64},{5,65},{6,66},{7,67},{8,76},{9,... | collective-permute-start | bytes 786440 | tf_op jit(solution)/shard_map/ppermute | solution.py:39
  217.8 8.1 %collective-permute-start.26 = (bf16[2,4,32,1024]{3,2,1,0:T(8,128)(2,1)S(1)}, bf16[2,4,32,1024]{3,2,1,0:T(8,128)(2,1)S(1)}, u32[]{:S(2)}, u32[]{:S(2)}) collective-permute-start(bf16[2,4,32,1024]{3,2,1,0:T(8,128)(2,1)S(1)} %get-tuple-element.31), channel_id=1, source_target_pairs={{0,1},{1,0},{2,3},{3,2},{4,5},{5,4},{6,7},{7,6},{8,24},{9,25},{10,... | collective-permute-start | bytes 1572872 | tf_op jit(solution)/shard_map/ppermute | solution.py:39
  217.9 14.7 %collective-permute-start.27 = (bf16[2,4,32,1024]{3,2,1,0:T(8,128)(2,1)S(1)}, bf16[2,4,32,1024]{3,2,1,0:T(8,128)(2,1)S(1)}, u32[]{:S(2)}, u32[]{:S(2)}) collective-permute-start(bf16[2,4,32,1024]{3,2,1,0:T(8,128)(2,1)S(1)} %get-tuple-element.33), channel_id=1, source_target_pairs={{0,2},{1,3},{2,0},{3,1},{4,6},{5,7},{6,4},{7,5},{8,40},{9,41},{10,... | collective-permute-start | bytes 1572872 | tf_op jit(solution)/shard_map/ppermute | solution.py:39
  220.4 16.3 %collective-permute-start.28 = (bf16[2,4,32,1024]{3,2,1,0:T(8,128)(2,1)S(1)}, bf16[2,4,32,1024]{3,2,1,0:T(8,128)(2,1)S(1)}, u32[]{:S(2)}, u32[]{:S(2)}) collective-permute-start(bf16[2,4,32,1024]{3,2,1,0:T(8,128)(2,1)S(1)} %get-tuple-element.32), channel_id=1, source_target_pairs={{0,3},{1,2},{2,1},{3,0},{4,7},{5,6},{6,5},{7,4},{8,56},{9,57},{10,... | collective-permute-start | bytes 1572872 | tf_op jit(solution)/shard_map/ppermute | solution.py:39
  221.9 18.0 %collective-permute-start.39 = (f32[2,16,1024]{2,1,0:T(8,128)S(1)}, f32[2,16,1024]{2,1,0:T(8,128)S(1)}, u32[]{:S(2)}, u32[]{:S(2)}) collective-permute-start(f32[2,16,1024]{2,1,0:T(8,128)S(1)} %get-tuple-element.42), channel_id=1, source_target_pairs={{0,16},{1,17},{2,18},{3,19},{4,20},{5,21},{6,22},{7,23},{8,24},{9,... | collective-permute-start | bytes 393224 | tf_op jit(solution)/shard_map/ppermute | solution.py:39
  222.0 19.0 %collective-permute-start.40 = (f32[2,16,1024]{2,1,0:T(8,128)S(1)}, f32[2,16,1024]{2,1,0:T(8,128)S(1)}, u32[]{:S(2)}, u32[]{:S(2)}) collective-permute-start(f32[2,16,1024]{2,1,0:T(8,128)S(1)} %get-tuple-element.44), channel_id=1, source_target_pairs={{0,32},{1,33},{2,34},{3,35},{4,36},{5,37},{6,38},{7,39},{8,40},{9,... | collective-permute-start | bytes 393224 | tf_op jit(solution)/shard_map/ppermute | solution.py:39
  225.9 15.1 %collective-permute-start.41 = (f32[2,16,1024]{2,1,0:T(8,128)S(1)}, f32[2,16,1024]{2,1,0:T(8,128)S(1)}, u32[]{:S(2)}, u32[]{:S(2)}) collective-permute-start(f32[2,16,1024]{2,1,0:T(8,128)S(1)} %get-tuple-element.43), channel_id=1, source_target_pairs={{0,48},{1,49},{2,50},{3,51},{4,52},{5,53},{6,54},{7,55},{8,56},{9,... | collective-permute-start | bytes 393224 | tf_op jit(solution)/shard_map/ppermute | solution.py:39
  237.0 5.3 %collective-permute-start.29 = (f32[2,32,1024]{2,1,0:T(8,128)S(1)}, f32[2,32,1024]{2,1,0:T(8,128)S(1)}, u32[]{:S(2)}, u32[]{:S(2)}) collective-permute-start(f32[2,32,1024]{2,1,0:T(8,128)S(1)} %get-tuple-element.36), channel_id=1, source_target_pairs={{0,4},{1,5},{2,6},{3,7},{4,0},{5,1},{6,2},{7,3},{8,9},{9,8},{10,11... | collective-permute-start | bytes 786440 | tf_op jit(solution)/shard_map/ppermute | solution.py:39
  237.1 9.5 %collective-permute-start.30 = (f32[2,32,1024]{2,1,0:T(8,128)S(1)}, f32[2,32,1024]{2,1,0:T(8,128)S(1)}, u32[]{:S(2)}, u32[]{:S(2)}) collective-permute-start(f32[2,32,1024]{2,1,0:T(8,128)S(1)} %get-tuple-element.38), channel_id=1, source_target_pairs={{0,64},{1,65},{2,66},{3,67},{4,68},{5,69},{6,70},{7,71},{8,10},{9,... | collective-permute-start | bytes 786440 | tf_op jit(solution)/shard_map/ppermute | solution.py:39
  240.0 9.2 %collective-permute-start.31 = (f32[2,32,1024]{2,1,0:T(8,128)S(1)}, f32[2,32,1024]{2,1,0:T(8,128)S(1)}, u32[]{:S(2)}, u32[]{:S(2)}) collective-permute-start(f32[2,32,1024]{2,1,0:T(8,128)S(1)} %get-tuple-element.37), channel_id=1, source_target_pairs={{0,68},{1,69},{2,70},{3,71},{4,64},{5,65},{6,66},{7,67},{8,11},{9,... | collective-permute-start | bytes 786440 | tf_op jit(solution)/shard_map/ppermute | solution.py:39
